TPU v7x, 32 devices: a whole 2x2x4 slice. The times are simulated.
32 devices in a mesh: groups: 2 (over x), seq: 16 (over z, y, core).
Axes of the slice: x: 2, y: 2, z: 4, core: 2. Of those that a mesh axis runs over, the one named last changes fastest.
Arguments:
- q_fresh: bfloat16 [5120, 4096], P(('groups', 'seq')), parts along dimension 0, may hold values from -9 to 9, as said below
- k_fresh: bfloat16 [5120, 4096], P(('groups', 'seq')), parts along dimension 0, may hold values from -5.6 to 5.6, as said below
- v_fresh: bfloat16 [5120, 4096], P(('groups', 'seq')), parts along dimension 0, may hold values from -6 to 6
- k_stale: bfloat16 [5120, 4096], P('groups', 'seq'), parts along dimension 0, may hold values from -5.59375 to 5.59375
- v_stale: bfloat16 [5120, 4096], P('groups', 'seq'), parts along dimension 0, may hold values from -6 to 6
- rank: int32 [10], P('groups'), parts along dimension 0, may hold values from 0 to 4, each once
- ends: int32 [10], P('groups'), parts along dimension 0, may hold values from 512 to 2560, as said below
Outputs:
- attended: bfloat16 [5120, 4096], P(('groups', 'seq')), parts along dimension 0
There are 2 independent parts, one for each index of `groups`. A program takes and returns all parts, laid end to end along the dimension named above; each array names one. Nothing has to cross between parts.
Inputs may be any that keep to these rules, and one draw needn't show every extreme that they name: `q_fresh`: queries of both draws lie within this range. `k_fresh`: keys of both draws lie within this range. Multiples of 512, never falling along the patches, ends[p] >= (p + 1) * 512; the first equals 512, the last equals 2560.
All inputs are finite; a program needn't handle non-finite values.
Results may differ from a plain program's by a relative error of at most 0.0036.
Values may be sent and summed in bfloat16 or wider, within the bound.
A program may use at most 64 MiB of HBM per device.

v0:
```python
import math

import jax
import jax.numpy as jnp
from jax import lax
from jax.sharding import PartitionSpec as P

HEAD_DIM = 128
PATCH = 512


def shards(q_fresh, k_fresh, v_fresh, k_stale, v_stale, rank, ends):
    queries, keys_new, values_new = (
        lax.all_to_all(q_fresh, "seq", split_axis=1, concat_axis=0, tiled=True),
        lax.all_to_all(k_fresh, "seq", split_axis=1, concat_axis=0, tiled=True),
        lax.all_to_all(v_fresh, "seq", split_axis=1, concat_axis=0, tiled=True),
    )
    total_rows = queries.shape[0]
    width = queries.shape[1]
    heads_here = width // HEAD_DIM
    patch_count = rank.shape[0]
    scale = 1.0 / math.sqrt(HEAD_DIM)
    key_patch = jnp.arange(total_rows, dtype=jnp.int32) // PATCH
    hits = key_patch[:, None] == jnp.arange(patch_count, dtype=jnp.int32)[None, :]
    key_rank = jnp.sum(jnp.where(hits, rank[None, :], 0), axis=1)
    positions = jnp.arange(total_rows, dtype=jnp.int32)

    def split_heads(array):
        return array.reshape(array.shape[0], heads_here, HEAD_DIM)

    def one_patch(index):
        block = split_heads(lax.dynamic_slice_in_dim(queries, index * PATCH, PATCH, 0))
        my_rank = rank[index]
        limit = ends[index]
        fresh = (key_rank <= my_rank)[:, None]
        keys = split_heads(jnp.where(fresh, keys_new, k_stale))
        values = split_heads(jnp.where(fresh, values_new, v_stale))
        score = jnp.einsum("qhd,khd->hqk", block, keys, preferred_element_type=jnp.float32) * scale
        score = jnp.where((positions < limit)[None, None, :], score, -jnp.inf)
        top = jnp.max(score, axis=2, keepdims=True)
        weight = jnp.exp(score - top)
        denominator = jnp.sum(weight, axis=2)
        mixed = jnp.einsum(
            "hqk,khd->qhd", weight.astype(jnp.bfloat16), values, preferred_element_type=jnp.float32
        )
        result = mixed / jnp.transpose(denominator)[:, :, None]
        return result.reshape(PATCH, width).astype(jnp.bfloat16)

    pieces = lax.map(one_patch, jnp.arange(patch_count, dtype=jnp.int32))
    gathered = pieces.reshape(total_rows, width)
    return lax.all_to_all(gathered, "seq", split_axis=0, concat_axis=1, tiled=True)


def solution(mesh):
    return jax.shard_map(
        shards,
        mesh=mesh,
        in_specs=(
            P(("groups", "seq"), None),
            P(("groups", "seq"), None),
            P(("groups", "seq"), None),
            P("groups", "seq"),
            P("groups", "seq"),
            P("groups"),
            P("groups"),
        ),
        out_specs=P(("groups", "seq"), None),
        check_vma=False,
    )
```

profile of v0, /device:TPU:13, one launch (start us, length us, event | category | flops | bytes accessed | tf_op | source)
XLA Modules:
  0.0 220.2 jit_solution(114587770779463893)
XLA Ops:
  0.0 2.5 %copy.83 = bf16[20,16,8,256]{3,2,0,1:T(8,128)(2,1)} copy(bf16[20,16,8,256]{3,2,1,0:T(8,128)(2,1)} %bitcast.75) | data formatting | bytes 2621440 | tf_op jit(solution)/shard_map/all_to_all | solution.py:16
  2.5 6.7 %all-to-all-start = ((bf16[160,16,256]{2,0,1:T(8,128)(2,1)}), bf16[160,16,256]{2,0,1:T(8,128)(2,1)S(1)}, u32[]{:S(2)}, u32[]{:S(2)}) async-start(bf16[160,16,256]{2,0,1:T(8,128)(2,1)} %bitcast.41), calls=%async_computation | async-start | bytes 2621440 | tf_op jit(solution)/shard_map/all_to_all | solution.py:16
  10.4 29.3 %all-to-all-done = bf16[160,16,256]{2,0,1:T(8,128)(2,1)S(1)} async-done(((bf16[160,16,256]{2,0,1:T(8,128)(2,1)}), bf16[160,16,256]{2,0,1:T(8,128)(2,1)S(1)}, u32[]{:S(2)}, u32[]{:S(2)}) %all-to-all-start) | async-done | bytes 1310752 | tf_op jit(solution)/shard_map/all_to_all | solution.py:16
  39.8 4.9 %all-to-all-start.2 = ((bf16[160,16,256]{2,0,1:T(8,128)(2,1)}), bf16[160,16,256]{2,0,1:T(8,128)(2,1)S(1)}, u32[]{:S(2)}, u32[]{:S(2)}) async-start(bf16[160,16,256]{2,0,1:T(8,128)(2,1)} %bitcast.73), calls=%async_computation.2 | async-start | bytes 2621440 | tf_op jit(solution)/shard_map/all_to_all | solution.py:15
  44.6 2.5 %copy.82 = bf16[20,16,8,256]{3,2,0,1:T(8,128)(2,1)} copy(bf16[20,16,8,256]{3,2,1,0:T(8,128)(2,1)} %bitcast.77) | data formatting | bytes 2621440 | tf_op jit(solution)/shard_map/all_to_all | solution.py:14
  47.1 28.1 %all-to-all-done.2 = bf16[160,16,256]{2,0,1:T(8,128)(2,1)S(1)} async-done(((bf16[160,16,256]{2,0,1:T(8,128)(2,1)}), bf16[160,16,256]{2,0,1:T(8,128)(2,1)S(1)}, u32[]{:S(2)}, u32[]{:S(2)}) %all-to-all-start.2) | async-done | bytes 1310752 | tf_op jit(solution)/shard_map/all_to_all | solution.py:15
  76.3 4.9 %all-to-all-start.1 = ((bf16[160,16,256]{2,0,1:T(8,128)(2,1)}), bf16[160,16,256]{2,0,1:T(8,128)(2,1)}, u32[]{:S(2)}, u32[]{:S(2)}) async-start(bf16[160,16,256]{2,0,1:T(8,128)(2,1)} %bitcast.72), calls=%async_computation.1 | async-start | bytes 2621440 | tf_op jit(solution)/shard_map/all_to_all | solution.py:14
  81.2 2.4 %copy.63 = bf16[2560,256]{0,1:T(8,128)(2,1)} copy(bf16[2560,256]{1,0:T(8,128)(2,1)} %param.13) | data formatting | bytes 2621440
  83.6 1.6 copy.66
  85.3 1.6 copy.62
  86.9 1.6 copy.65
  88.6 23.3 %all-to-all-done.1 = bf16[160,16,256]{2,0,1:T(8,128)(2,1)} async-done(((bf16[160,16,256]{2,0,1:T(8,128)(2,1)}), bf16[160,16,256]{2,0,1:T(8,128)(2,1)}, u32[]{:S(2)}, u32[]{:S(2)}) %all-to-all-start.1) | async-done | bytes 1310752 | tf_op jit(solution)/shard_map/all_to_all | solution.py:14
  111.8 71.8 %while.11 = (s32[]{:T(128)}, bf16[5,512,256]{2,1,0:T(8,128)(2,1)}, s32[5]{0:T(128)S(1)}, s32[5]{0:T(128)S(1)}, s32[2560]{0:T(1024)S(1)}, /*index=5*/bf16[2560,25...) while((s32[]{:T(128)}, bf16[5,512,256]{2,1,0:T(8,128)(2,1)}, ...), condition=%wide.region_4.5_spmd.clone, body=%wide.region_1.4_spmd.clone.sunk | while | flops 1372589056 | bytes 49856844 | solution.py:49
  115.6 1.3 iota_compare_fusion.3
  118.6 1.7 fusion.43
  120.4 2.2 %fusion.44 = f32[2,512]{1,0:T(2,128)S(1)} fusion(f32[2,512,2560]{2,1,0:T(8,128)S(1)} %get-tuple-element.257, f32[2,512]{1,0:T(2,128)S(1)} %get-tuple-element.258, pred[2560]{0:T(1024)(128)(4,1)S(1)} %get-tuple-element.255), kind=kLoop, calls=%fused_computation.4.clone.1 | loop fusion | flops 10484736 | bytes 10496512 | tf_op jit(solution)/shard_map/while/body/eval_jaxpr/reduce_sum | solution.py:42
  122.6 2.7 %fusion.45 = bf16[512,2,128]{0,2,1:T(8,128)(2,1)S(1)} fusion(f32[2,512,2560]{2,1,0:T(8,128)S(1)} %get-tuple-element.257, f32[2,512]{1,0:T(2,128)S(1)} %get-tuple-element.258, pred[2560]{0:T(1024)(128)(4,1)S(1)} %get-tuple-element.255, bf16[2560,2,128]{0,2,1:T(8,128)(2,1)S(1)} %bitcast.79, bf16[2560,2,128]{0,2,1:T(8,128)(2,1)S(1)} %bitcast.78, ...), kind=kOutput, calls=%fused_computation.15.clone.1 | convolution fusion | flops 682491904 | bytes 13382656 | tf_op jit(solution)/shard_map/while/body/eval_jaxpr/hqk,khd->qhd/dot_general | solution.py:43
  130.0 1.3 iota_compare_fusion.3
  133.0 1.7 fusion.43
  134.7 2.2 %fusion.44 = f32[2,512]{1,0:T(2,128)S(1)} fusion(f32[2,512,2560]{2,1,0:T(8,128)S(1)} %get-tuple-element.257, f32[2,512]{1,0:T(2,128)S(1)} %get-tuple-element.258, pred[2560]{0:T(1024)(128)(4,1)S(1)} %get-tuple-element.255), kind=kLoop, calls=%fused_computation.4.clone.1 | loop fusion | flops 10484736 | bytes 10496512 | tf_op jit(solution)/shard_map/while/body/eval_jaxpr/reduce_sum | solution.py:42
  137.0 2.7 %fusion.45 = bf16[512,2,128]{0,2,1:T(8,128)(2,1)S(1)} fusion(f32[2,512,2560]{2,1,0:T(8,128)S(1)} %get-tuple-element.257, f32[2,512]{1,0:T(2,128)S(1)} %get-tuple-element.258, pred[2560]{0:T(1024)(128)(4,1)S(1)} %get-tuple-element.255, bf16[2560,2,128]{0,2,1:T(8,128)(2,1)S(1)} %bitcast.79, bf16[2560,2,128]{0,2,1:T(8,128)(2,1)S(1)} %bitcast.78, ...), kind=kOutput, calls=%fused_computation.15.clone.1 | convolution fusion | flops 682491904 | bytes 13382656 | tf_op jit(solution)/shard_map/while/body/eval_jaxpr/hqk,khd->qhd/dot_general | solution.py:43
  144.3 1.3 iota_compare_fusion.3
  147.4 1.7 fusion.43
  149.1 2.2 %fusion.44 = f32[2,512]{1,0:T(2,128)S(1)} fusion(f32[2,512,2560]{2,1,0:T(8,128)S(1)} %get-tuple-element.257, f32[2,512]{1,0:T(2,128)S(1)} %get-tuple-element.258, pred[2560]{0:T(1024)(128)(4,1)S(1)} %get-tuple-element.255), kind=kLoop, calls=%fused_computation.4.clone.1 | loop fusion | flops 10484736 | bytes 10496512 | tf_op jit(solution)/shard_map/while/body/eval_jaxpr/reduce_sum | solution.py:42
  151.4 2.7 %fusion.45 = bf16[512,2,128]{0,2,1:T(8,128)(2,1)S(1)} fusion(f32[2,512,2560]{2,1,0:T(8,128)S(1)} %get-tuple-element.257, f32[2,512]{1,0:T(2,128)S(1)} %get-tuple-element.258, pred[2560]{0:T(1024)(128)(4,1)S(1)} %get-tuple-element.255, bf16[2560,2,128]{0,2,1:T(8,128)(2,1)S(1)} %bitcast.79, bf16[2560,2,128]{0,2,1:T(8,128)(2,1)S(1)} %bitcast.78, ...), kind=kOutput, calls=%fused_computation.15.clone.1 | convolution fusion | flops 682491904 | bytes 13382656 | tf_op jit(solution)/shard_map/while/body/eval_jaxpr/hqk,khd->qhd/dot_general | solution.py:43
  161.7 1.7 fusion.43
  163.5 2.2 %fusion.44 = f32[2,512]{1,0:T(2,128)S(1)} fusion(f32[2,512,2560]{2,1,0:T(8,128)S(1)} %get-tuple-element.257, f32[2,512]{1,0:T(2,128)S(1)} %get-tuple-element.258, pred[2560]{0:T(1024)(128)(4,1)S(1)} %get-tuple-element.255), kind=kLoop, calls=%fused_computation.4.clone.1 | loop fusion | flops 10484736 | bytes 10496512 | tf_op jit(solution)/shard_map/while/body/eval_jaxpr/reduce_sum | solution.py:42
  165.7 2.7 %fusion.45 = bf16[512,2,128]{0,2,1:T(8,128)(2,1)S(1)} fusion(f32[2,512,2560]{2,1,0:T(8,128)S(1)} %get-tuple-element.257, f32[2,512]{1,0:T(2,128)S(1)} %get-tuple-element.258, pred[2560]{0:T(1024)(128)(4,1)S(1)} %get-tuple-element.255, bf16[2560,2,128]{0,2,1:T(8,128)(2,1)S(1)} %bitcast.79, bf16[2560,2,128]{0,2,1:T(8,128)(2,1)S(1)} %bitcast.78, ...), kind=kOutput, calls=%fused_computation.15.clone.1 | convolution fusion | flops 682491904 | bytes 13382656 | tf_op jit(solution)/shard_map/while/body/eval_jaxpr/hqk,khd->qhd/dot_general | solution.py:43
  176.1 1.7 fusion.43
  177.8 2.2 %fusion.44 = f32[2,512]{1,0:T(2,128)S(1)} fusion(f32[2,512,2560]{2,1,0:T(8,128)S(1)} %get-tuple-element.257, f32[2,512]{1,0:T(2,128)S(1)} %get-tuple-element.258, pred[2560]{0:T(1024)(128)(4,1)S(1)} %get-tuple-element.255), kind=kLoop, calls=%fused_computation.4.clone.1 | loop fusion | flops 10484736 | bytes 10496512 | tf_op jit(solution)/shard_map/while/body/eval_jaxpr/reduce_sum | solution.py:42
  180.1 2.7 %fusion.45 = bf16[512,2,128]{0,2,1:T(8,128)(2,1)S(1)} fusion(f32[2,512,2560]{2,1,0:T(8,128)S(1)} %get-tuple-element.257, f32[2,512]{1,0:T(2,128)S(1)} %get-tuple-element.258, pred[2560]{0:T(1024)(128)(4,1)S(1)} %get-tuple-element.255, bf16[2560,2,128]{0,2,1:T(8,128)(2,1)S(1)} %bitcast.79, bf16[2560,2,128]{0,2,1:T(8,128)(2,1)S(1)} %bitcast.78, ...), kind=kOutput, calls=%fused_computation.15.clone.1 | convolution fusion | flops 682491904 | bytes 13382656 | tf_op jit(solution)/shard_map/while/body/eval_jaxpr/hqk,khd->qhd/dot_general | solution.py:43
  183.7 35.3 %all_to_all.76 = bf16[16,160,256]{2,1,0:T(8,128)(2,1)S(1)} all-to-all(bf16[16,160,256]{2,1,0:T(8,128)(2,1)} %bitcast.80), channel_id=1, replica_groups=mesh['groups'=2,'seq'=16] {'seq'}, dimensions={0} | all-to-all | bytes 2621440 | tf_op jit(solution)/shard_map/all_to_all | solution.py:51
  (71 shorter events, 25.6 us)
Async XLA Ops:
  2.5 6.7 %copy-start.1 = (bf16[160,4096]{1,0:T(8,128)(2,1)S(1)}, bf16[160,4096]{1,0:T(8,128)(2,1)}, u32[]{:S(2)}) copy-start(bf16[160,4096]{1,0:T(8,128)(2,1)} %param.10) | copy-start | bytes 3932164
  2.5 37.3 %all-to-all-start = ((bf16[160,16,256]{2,0,1:T(8,128)(2,1)}), bf16[160,16,256]{2,0,1:T(8,128)(2,1)S(1)}, u32[]{:S(2)}, u32[]{:S(2)}) async-start(bf16[160,16,256]{2,0,1:T(8,128)(2,1)} %bitcast.41), calls=%async_computation | async-start | bytes 2621440 | tf_op jit(solution)/shard_map/all_to_all | solution.py:16
  39.8 35.4 %all-to-all-start.2 = ((bf16[160,16,256]{2,0,1:T(8,128)(2,1)}), bf16[160,16,256]{2,0,1:T(8,128)(2,1)S(1)}, u32[]{:S(2)}, u32[]{:S(2)}) async-start(bf16[160,16,256]{2,0,1:T(8,128)(2,1)} %bitcast.73), calls=%async_computation.2 | async-start | bytes 2621440 | tf_op jit(solution)/shard_map/all_to_all | solution.py:15
  75.2 1.1 copy-start
  76.3 35.5 %all-to-all-start.1 = ((bf16[160,16,256]{2,0,1:T(8,128)(2,1)}), bf16[160,16,256]{2,0,1:T(8,128)(2,1)}, u32[]{:S(2)}, u32[]{:S(2)}) async-start(bf16[160,16,256]{2,0,1:T(8,128)(2,1)} %bitcast.72), calls=%async_computation.1 | async-start | bytes 2621440 | tf_op jit(solution)/shard_map/all_to_all | solution.py:14
  83.6 1.6 copy-start.4
  86.9 24.9 %copy-start.5 = (s32[5]{0:T(128)S(1)}, s32[5]{0:T(128)}, u32[]{:S(2)}) copy-start(s32[5]{0:T(128)} %param.15) | copy-start | bytes 64
  120.4 2.3 %copy-start.2 = (bf16[2560,256]{0,1:T(8,128)(2,1)S(1)}, bf16[2560,256]{0,1:T(8,128)(2,1)}, u32[]{:S(2)}) copy-start(bf16[2560,256]{0,1:T(8,128)(2,1)} %get-tuple-element.297) | copy-start | bytes 3932164 | tf_op jit(solution)/shard_map/while
  120.4 2.3 %copy-start.3 = (bf16[2560,256]{0,1:T(8,128)(2,1)S(1)}, bf16[2560,256]{0,1:T(8,128)(2,1)}, u32[]{:S(2)}) copy-start(bf16[2560,256]{0,1:T(8,128)(2,1)} %get-tuple-element.296) | copy-start | bytes 3932164 | tf_op jit(solution)/shard_map/while
  134.7 2.3 %copy-start.2 = (bf16[2560,256]{0,1:T(8,128)(2,1)S(1)}, bf16[2560,256]{0,1:T(8,128)(2,1)}, u32[]{:S(2)}) copy-start(bf16[2560,256]{0,1:T(8,128)(2,1)} %get-tuple-element.297) | copy-start | bytes 3932164 | tf_op jit(solution)/shard_map/while
  134.7 2.3 %copy-start.3 = (bf16[2560,256]{0,1:T(8,128)(2,1)S(1)}, bf16[2560,256]{0,1:T(8,128)(2,1)}, u32[]{:S(2)}) copy-start(bf16[2560,256]{0,1:T(8,128)(2,1)} %get-tuple-element.296) | copy-start | bytes 3932164 | tf_op jit(solution)/shard_map/while
  149.1 2.3 %copy-start.2 = (bf16[2560,256]{0,1:T(8,128)(2,1)S(1)}, bf16[2560,256]{0,1:T(8,128)(2,1)}, u32[]{:S(2)}) copy-start(bf16[2560,256]{0,1:T(8,128)(2,1)} %get-tuple-element.297) | copy-start | bytes 3932164 | tf_op jit(solution)/shard_map/while
  149.1 2.3 %copy-start.3 = (bf16[2560,256]{0,1:T(8,128)(2,1)S(1)}, bf16[2560,256]{0,1:T(8,128)(2,1)}, u32[]{:S(2)}) copy-start(bf16[2560,256]{0,1:T(8,128)(2,1)} %get-tuple-element.296) | copy-start | bytes 3932164 | tf_op jit(solution)/shard_map/while
  163.5 2.3 %copy-start.2 = (bf16[2560,256]{0,1:T(8,128)(2,1)S(1)}, bf16[2560,256]{0,1:T(8,128)(2,1)}, u32[]{:S(2)}) copy-start(bf16[2560,256]{0,1:T(8,128)(2,1)} %get-tuple-element.297) | copy-start | bytes 3932164 | tf_op jit(solution)/shard_map/while
  163.5 2.3 %copy-start.3 = (bf16[2560,256]{0,1:T(8,128)(2,1)S(1)}, bf16[2560,256]{0,1:T(8,128)(2,1)}, u32[]{:S(2)}) copy-start(bf16[2560,256]{0,1:T(8,128)(2,1)} %get-tuple-element.296) | copy-start | bytes 3932164 | tf_op jit(solution)/shard_map/while
  177.8 2.3 %copy-start.2 = (bf16[2560,256]{0,1:T(8,128)(2,1)S(1)}, bf16[2560,256]{0,1:T(8,128)(2,1)}, u32[]{:S(2)}) copy-start(bf16[2560,256]{0,1:T(8,128)(2,1)} %get-tuple-element.297) | copy-start | bytes 3932164 | tf_op jit(solution)/shard_map/while
  177.8 2.3 %copy-start.3 = (bf16[2560,256]{0,1:T(8,128)(2,1)S(1)}, bf16[2560,256]{0,1:T(8,128)(2,1)}, u32[]{:S(2)}) copy-start(bf16[2560,256]{0,1:T(8,128)(2,1)} %get-tuple-element.296) | copy-start | bytes 3932164 | tf_op jit(solution)/shard_map/while
where the time goes:
time: 223 us; the launch traced here: 220 us
  waiting for transfers between devices  80.7 us (36%)
  blocking collectives  35.3 us (16%)
  local copies, waits for them, and re-layouts  35.2 us (16%)
  matrix products  22.2 us (10%)
  other arithmetic  17.6 us (8%)
  starting transfers between devices  16.4 us (7%)
  loops' own time  12.7 us (6%)
    all_to_all x1, blocking collectives, shards(): lax.all_to_all(gathered, 'seq', split_axis=0, concat_axis=1, tiled=True)  35.3 us
    all_to_all x1, waiting for transfers between devices, shards(): lax.all_to_all(v_fresh, 'seq', split_axis=1, concat_axis=0, tiled=True)  29.3 us
    all_to_all x1, waiting for transfers between devices, shards(): lax.all_to_all(k_fresh, 'seq', split_axis=1, concat_axis=0, tiled=True)  28.1 us
    all_to_all x1, waiting for transfers between devices, shards(): lax.all_to_all(q_fresh, 'seq', split_axis=1, concat_axis=0, tiled=True)  23.3 us
    dot_general x5, matrix products, one_patch(): jnp.einsum('hqk,khd->qhd', weight.astype(jnp.bfloat16), values, preferred...  13.6 us
    another operation x1, loops' own time, shards(): pieces = lax.map(one_patch, jnp.arange(patch_count, dtype=jnp.int32))  12.7 us
    reduce_sum x5, other arithmetic, one_patch(): denominator = jnp.sum(weight, axis=2)  11.2 us
    dot_general x5, matrix products, one_patch(): jnp.einsum('qhd,khd->hqk', block, keys, preferred_element_type=jnp.float32)  8.59 us
  transfers between devices with their start and end apart: 3, of which 3 were waited for; matrix products, arithmetic and copies ran while one was open for 5% of the time, Pallas kernels for 0%

commit v1 on v0

v1 whole, which is shorter than its diff:
```python
import functools
import math

import jax
import jax.numpy as jnp
from jax import lax
from jax.experimental import pallas as pl
from jax.experimental.pallas import tpu as pltpu
from jax.sharding import PartitionSpec as P

HEAD_DIM = 128
PATCH = 512
TILE = 256
HIDDEN = -1e30


def attend(patch, keys_of, blocks, rank, ends, q, k, v, o):
    factor = math.log2(math.e) / math.sqrt(HEAD_DIM)
    for part in range(PATCH // TILE):
        rows = pl.ds(pl.multiple_of(patch * PATCH + part * TILE, TILE), TILE)
        query = q[rows, :]
        top = None
        for block in range(blocks):
            stale = keys_of(block)
            span = pl.ds(block * PATCH, PATCH)
            key = k[stale, span, :]
            value = v[stale, span, :]
            score = lax.dot_general(
                query, key, (((1,), (1,)), ((), ())), preferred_element_type=jnp.float32
            )
            shift = jnp.where(block * PATCH < ends[patch], 0.0, HIDDEN).astype(jnp.float32)
            high = jnp.max(score, axis=1, keepdims=True) * factor + shift
            new_top = high if top is None else jnp.maximum(top, high)
            weight = jnp.exp2(score * factor - (new_top - shift)).astype(jnp.bfloat16)
            wide = jnp.concatenate([value, jnp.ones_like(value)], axis=1)
            mixed = jnp.dot(weight, wide, preferred_element_type=jnp.float32)
            if top is None:
                total = mixed
            else:
                total = total * jnp.exp2(top - new_top) + mixed
            top = new_top
        o[rows, :] = (total[:, :HEAD_DIM] / total[:, HEAD_DIM:]).astype(o.dtype)


def kernel(n, heads, q_in, k_in, v_in, ks_in, vs_in, rank, ends, out, *scratch):
    bufs = [scratch[4 * h : 4 * h + 4] for h in range(heads)]
    send_sem, recv_sem, out_send, out_recv = scratch[4 * heads :]
    rows = q_in.shape[0]
    width = heads * HEAD_DIM
    patches = rank.shape[0]
    me = lax.axis_index("seq")
    barrier = pltpu.get_barrier_semaphore()

    def greet(step, carry):
        pl.semaphore_signal(barrier, inc=1, device_id={"seq": lax.rem(me + step, n)})
        return carry

    lax.fori_loop(1, n, greet, 0)
    own_rows = pl.ds(pl.multiple_of(me * rows, rows), rows)

    def columns(device, head):
        return pl.ds(pl.multiple_of(device * width + head * HEAD_DIM, HEAD_DIM), HEAD_DIM)

    plan = []
    for head in range(heads):
        q, k, v, o = bufs[head]
        own = pl.ds(head * HEAD_DIM, HEAD_DIM)
        pltpu.make_async_copy(ks_in.at[:, own], k.at[1], recv_sem.at[head, 0]).start()
        pltpu.make_async_copy(vs_in.at[:, own], v.at[1], recv_sem.at[head, 1]).start()
        plan.append((head, 0, k_in, k.at[0, own_rows]))
        plan.append((head, 1, v_in, v.at[0, own_rows]))
        plan.append((head, 2, q_in, q.at[own_rows]))
    for head, kind, source, target in plan:
        pltpu.make_async_copy(
            source.at[:, columns(me, head)], target, recv_sem.at[head, kind]
        ).start()
    pl.semaphore_wait(barrier, n - 1)
    for head, kind, source, target in plan:

        def send(step, carry, head=head, kind=kind, source=source, target=target):
            peer = lax.rem(me + step, n)
            pltpu.make_async_remote_copy(
                src_ref=source.at[:, columns(peer, head)],
                dst_ref=target,
                send_sem=send_sem.at[head, kind],
                recv_sem=recv_sem.at[head, kind],
                device_id={"seq": peer},
            ).start()
            return carry

        lax.fori_loop(1, n, send, 0)

    for head in range(heads):
        q, k, v, o = bufs[head]

        def wait_for(ref, sem):
            pltpu.make_async_copy(ref, ref, sem).wait()

        wait_for(k, recv_sem.at[head, 0])
        wait_for(v, recv_sem.at[head, 1])
        wait_for(q, recv_sem.at[head, 2])

        def send_out(block, carry, head=head, o=o):
            source = o.at[pl.ds(pl.multiple_of(block * rows, rows), rows)]
            target = out.at[:, columns(me, head)]

            @pl.when(block == me)
            def _():
                pltpu.make_async_copy(source, target, out_recv).start()

            @pl.when(block != me)
            def _():
                pltpu.make_async_remote_copy(
                    src_ref=source,
                    dst_ref=target,
                    send_sem=out_send.at[head],
                    recv_sem=out_recv,
                    device_id={"seq": block},
                ).start()

            return carry

        attend(0, lambda block: 0, 1, rank, ends, q, k, v, o)
        lax.fori_loop(0, PATCH // rows, send_out, 0)

        def one_patch(patch, carry, q=q, k=k, v=v, o=o, send_out=send_out):
            mine = rank[patch]
            attend(
                patch,
                lambda block: (rank[block] > mine).astype(jnp.int32),
                patches,
                rank,
                ends,
                q,
                k,
                v,
                o,
            )
            lax.fori_loop(patch * PATCH // rows, (patch + 1) * PATCH // rows, send_out, 0)
            return carry

        lax.fori_loop(1, patches, one_patch, 0)

    others = pl.ds(0, (n - 1) * rows)
    for head in range(heads):
        q, k, v, o = bufs[head]
        for kind in range(3):
            part = q.at[others]
            pltpu.make_async_copy(part, part, send_sem.at[head, kind]).wait()
        part = o.at[others]
        pltpu.make_async_copy(part, part, out_send.at[head]).wait()
    pltpu.make_async_copy(out, out, out_recv).wait()


def shards(n, q_fresh, k_fresh, v_fresh, k_stale, v_stale, rank, ends):
    rows, whole_width = q_fresh.shape
    heads = whole_width // n // HEAD_DIM
    span = n * rows
    any_spec = pl.BlockSpec(memory_space=pl.ANY)
    smem_spec = pl.BlockSpec(memory_space=pltpu.SMEM)
    scratch = []
    for _ in range(heads):
        scratch += [
            pltpu.VMEM((span, HEAD_DIM), jnp.bfloat16),
            pltpu.VMEM((2, span, HEAD_DIM), jnp.bfloat16),
            pltpu.VMEM((2, span, HEAD_DIM), jnp.bfloat16),
            pltpu.VMEM((span, HEAD_DIM), jnp.bfloat16),
        ]
    scratch += [
        pltpu.SemaphoreType.DMA((heads, 3)),
        pltpu.SemaphoreType.DMA((heads, 3)),
        pltpu.SemaphoreType.DMA((heads,)),
        pltpu.SemaphoreType.DMA,
    ]
    return pl.pallas_call(
        functools.partial(kernel, n, heads),
        out_shape=jax.ShapeDtypeStruct(q_fresh.shape, q_fresh.dtype),
        in_specs=[any_spec] * 5 + [smem_spec] * 2,
        out_specs=any_spec,
        scratch_shapes=scratch,
        compiler_params=pltpu.CompilerParams(
            collective_id=0, has_side_effects=True, vmem_limit_bytes=48 * 1024 * 1024
        ),
        cost_estimate=pl.CostEstimate(
            flops=4 * heads * span * span * HEAD_DIM,
            bytes_accessed=12 * rows * whole_width,
            transcendentals=heads * span * span,
        ),
    )(q_fresh, k_fresh, v_fresh, k_stale, v_stale, rank, ends)


def solution(mesh):
    return jax.shard_map(
        functools.partial(shards, mesh.shape["seq"]),
        mesh=mesh,
        in_specs=(
            P(("groups", "seq"), None),
            P(("groups", "seq"), None),
            P(("groups", "seq"), None),
            P("groups", "seq"),
            P("groups", "seq"),
            P("groups"),
            P("groups"),
        ),
        out_specs=P(("groups", "seq"), None),
        check_vma=False,
    )
```

time: 223 us -> 125 us (0.56); the launches traced: 220 us -> 125 us
  Pallas kernels: 0 us -> 118 us
  waiting for transfers between devices: 80.7 us -> 0 us
  blocking collectives: 35.3 us -> 0 us
  local copies, waits for them, and re-layouts: 35.2 us -> 6.32 us
  matrix products: 22.2 us -> 0 us
  other arithmetic: 17.6 us -> 0 us
  starting transfers between devices: 16.4 us -> 0 us
  loops' own time: 12.7 us -> 0 us
    pallas_call x0 -> x1, Pallas kernels: none -> 118 us  [shards(): pl.pallas_call(functools.partial(kernel, n, heads), out_shape=jax.ShapeDt...]
    all_to_all x3 -> x0, waiting for transfers between devices: 80.7 us -> none  [the longest x1 29.3 us: shards(): lax.all_to_all(v_fresh, 'seq', split_axis=1, concat_axis=0, tiled=True)]
    all_to_all x1 -> x0, blocking collectives: 35.3 us -> none  [shards(): lax.all_to_all(gathered, 'seq', split_axis=0, concat_axis=1, tiled=True)]
    dot_general x10 -> x0, matrix products: 22.2 us -> none  [the longest x5 13.6 us: one_patch(): jnp.einsum('hqk,khd->qhd', weight.astype(jnp.bfloat16), values, preferred...]
    all_to_all x3 -> x0, starting transfers between devices: 16.4 us -> none  [the longest x1 6.69 us: shards(): lax.all_to_all(v_fresh, 'seq', split_axis=1, concat_axis=0, tiled=True)]
    dynamic_slice x25 -> x0, local copies, waits for them, and re-layouts: 15.1 us -> none  [the longest x10 5.57 us: one_patch(): lax.dynamic_slice_in_dim(queries, index * PATCH, PATCH, 0)]
    another operation x1 -> x0, loops' own time: 12.7 us -> none  [shards(): pieces = lax.map(one_patch, jnp.arange(patch_count, dtype=jnp.int32))]
    reduce_sum x6 -> x0, other arithmetic: 11.3 us -> none  [the longest x5 11.2 us: one_patch(): denominator = jnp.sum(weight, axis=2)]
  transfers between devices with their start and end apart: 3 -> 0, of which waited for: 3 -> 0; matrix products, arithmetic and copies ran while one was open for 5% -> 0% of each run, Pallas kernels for 0% -> 0%
where the time goes in v1:
time: 125 us
  Pallas kernels  118 us (94%)
  local copies, waits for them, and re-layouts  6.32 us (5%)
    pallas_call x1, Pallas kernels, shards(): pl.pallas_call(functools.partial(kernel, n, heads), out_shape=jax.ShapeDt...  118 us
    unnamed x11, local copies, waits for them, and re-layouts  6.32 us

profile of v1, /device:TPU:13, one launch (start us, length us, event | category | flops | bytes accessed | tf_op | source)
XLA Modules:
  0.0 124.8 jit_solution(6640689298127322207)
XLA Ops:
  0.0 0.0 copy-start
  0.0 1.3 %copy-done = bf16[160,4096]{1,0:T(8,128)(2,1)S(1)} copy-done((bf16[160,4096]{1,0:T(8,128)(2,1)S(1)}, bf16[160,4096]{1,0:T(8,128)(2,1)}, u32[]{:S(2)}) %copy-start) | copy-done | bytes 1310744
  1.3 0.0 copy-start.1
  1.3 1.3 %copy-done.1 = bf16[160,4096]{1,0:T(8,128)(2,1)S(1)} copy-done((bf16[160,4096]{1,0:T(8,128)(2,1)S(1)}, bf16[160,4096]{1,0:T(8,128)(2,1)}, u32[]{:S(2)}) %copy-start.1) | copy-done | bytes 1310744
  2.6 0.0 copy-start.2
  2.6 1.3 %copy-done.2 = bf16[160,4096]{1,0:T(8,128)(2,1)S(1)} copy-done((bf16[160,4096]{1,0:T(8,128)(2,1)S(1)}, bf16[160,4096]{1,0:T(8,128)(2,1)}, u32[]{:S(2)}) %copy-start.2) | copy-done | bytes 1310744
  4.0 0.0 copy-start.3
  4.0 0.7 copy-done.3
  4.6 0.0 copy-start.4
  4.6 0.7 copy-done.4
  5.3 118.4 %shard_map.73 = bf16[160,4096]{1,0:T(8,128)(2,1)S(1)} custom-call(bf16[160,4096]{1,0:T(8,128)(2,1)S(1)} %copy-done, bf16[160,4096]{1,0:T(8,128)(2,1)S(1)} %copy-done.1, bf16[160,4096]{1,0:T(8,128)(2,1)S(1)} %copy-done.2, bf16[2560,256]{1,0:T(8,128)(2,1)} %ks_in.1, bf16[2560,256]{1,0:T(8,128)(2,1)} %vs_in.1, s32[5]{0:T(128)S(1)} %copy-done.3, s32[5]{0:T(128)S(1)} %copy-done.4), custom_call_target="tpu_custom_call" | custom-call | flops 6710886400 | bytes 7864320 | tf_op jit(solution)/shard_map/pallas_call | solution.py:175
  123.7 1.1 copy.9
Async XLA Ops:
  0.0 1.3 %copy-start = (bf16[160,4096]{1,0:T(8,128)(2,1)S(1)}, bf16[160,4096]{1,0:T(8,128)(2,1)}, u32[]{:S(2)}) copy-start(bf16[160,4096]{1,0:T(8,128)(2,1)} %q_in.1) | copy-start | bytes 3932164
  1.3 1.3 %copy-start.1 = (bf16[160,4096]{1,0:T(8,128)(2,1)S(1)}, bf16[160,4096]{1,0:T(8,128)(2,1)}, u32[]{:S(2)}) copy-start(bf16[160,4096]{1,0:T(8,128)(2,1)} %k_in.1) | copy-start | bytes 3932164
  2.6 1.3 %copy-start.2 = (bf16[160,4096]{1,0:T(8,128)(2,1)S(1)}, bf16[160,4096]{1,0:T(8,128)(2,1)}, u32[]{:S(2)}) copy-start(bf16[160,4096]{1,0:T(8,128)(2,1)} %v_in.1) | copy-start | bytes 3932164
  4.0 0.7 copy-start.3
  4.6 0.7 copy-start.4

commit v2 on v1

v2 whole, which is shorter than its diff:
```python
import functools
import math

import jax
import jax.numpy as jnp
from jax import lax
from jax.experimental import pallas as pl
from jax.experimental.pallas import tpu as pltpu
from jax.sharding import PartitionSpec as P

HEAD_DIM = 128
PATCH = 512
TILE = 256
HIDDEN = -1e30


def attend(patch, keys_of, blocks, rank, ends, q, k, v, o):
    factor = math.log2(math.e) / math.sqrt(HEAD_DIM)
    for part in range(PATCH // TILE):
        rows = pl.ds(pl.multiple_of(patch * PATCH + part * TILE, TILE), TILE)
        query = q[rows, :]
        top = None
        for block in range(blocks):
            stale = keys_of(block)
            span = pl.ds(block * PATCH, PATCH)
            key = k[stale, span, :]
            value = v[stale, span, :]
            score = lax.dot_general(
                query, key, (((1,), (1,)), ((), ())), preferred_element_type=jnp.float32
            )
            shift = jnp.where(block * PATCH < ends[patch], 0.0, HIDDEN).astype(jnp.float32)
            high = jnp.max(score, axis=1, keepdims=True) * factor + shift
            new_top = high if top is None else jnp.maximum(top, high)
            weight = jnp.exp2(score * factor - (new_top - shift)).astype(jnp.bfloat16)
            wide = jnp.concatenate([value, jnp.ones_like(value)], axis=1)
            mixed = jnp.dot(weight, wide, preferred_element_type=jnp.float32)
            if top is None:
                total = mixed
            else:
                total = total * jnp.exp2(top - new_top) + mixed
            top = new_top
        o[rows, :] = (total[:, :HEAD_DIM] / total[:, HEAD_DIM:]).astype(o.dtype)


def kernel(n, heads, q_in, k_in, v_in, ks_in, vs_in, rank_in, ends_in, out, *scratch):
    bufs = [scratch[8 * h : 8 * h + 8] for h in range(heads)]
    rank, ends, small_sem, send_sem, recv_sem, x_send, x_recv, out_send, xo_send, out_recv = scratch[
        8 * heads :
    ]
    rows = q_in.shape[0]
    width = heads * HEAD_DIM
    patches = rank.shape[0]
    half = n // 2
    full, rest = divmod(PATCH, rows)
    owners = full + (1 if rest else 0)
    me = lax.axis_index("seq")
    lower = me < half
    barrier = pltpu.get_barrier_semaphore()

    def greet(step, carry):
        pl.semaphore_signal(barrier, inc=1, device_id={"seq": lax.rem(me + step, n)})
        return carry

    lax.fori_loop(1, n, greet, 0)
    own_rows = pl.ds(pl.multiple_of(me * rows, rows), rows)

    def columns(device, head):
        return pl.ds(pl.multiple_of(device * width + head * HEAD_DIM, HEAD_DIM), HEAD_DIM)

    def local(source, target, sem):
        pltpu.make_async_copy(source, target, sem).start()

    def remote(source, target, away, here, peer):
        pltpu.make_async_remote_copy(
            src_ref=source,
            dst_ref=target,
            send_sem=away,
            recv_sem=here,
            device_id={"seq": peer},
        ).start()

    def wait_for(ref, sem):
        pltpu.make_async_copy(ref, ref, sem).wait()

    local(rank_in, rank, small_sem.at[0])
    local(ends_in, ends, small_sem.at[1])
    for head in range(heads):
        q, k, v = bufs[head][:3]
        own = pl.ds(head * HEAD_DIM, HEAD_DIM)
        local(ks_in.at[:, own], k.at[1], recv_sem.at[head, 0])
        local(vs_in.at[:, own], v.at[1], recv_sem.at[head, 1])
        mine = columns(me, head)
        local(k_in.at[:, mine], k.at[0, own_rows], recv_sem.at[head, 0])
        local(v_in.at[:, mine], v.at[0, own_rows], recv_sem.at[head, 1])
        local(q_in.at[:, mine], q.at[own_rows], recv_sem.at[head, 2])
    pl.semaphore_wait(barrier, n - 1)

    def send_head(head):
        q, k, v = bufs[head][:3]
        for kind, source, target in ((0, k_in, k), (1, v_in, v)):

            def send(step, carry, kind=kind, source=source, target=target):
                peer = lax.rem(me + step, n)
                remote(
                    source.at[:, columns(peer, head)],
                    target.at[0, own_rows],
                    send_sem.at[head, kind],
                    recv_sem.at[head, kind],
                    peer,
                )
                return carry

            lax.fori_loop(1, n, send, 0)

        def send_query(step, carry):
            peer = lax.rem(me + step, n)
            sems = (send_sem.at[head, 2], recv_sem.at[head, 2], peer)

            @pl.when((peer < half) | (me >= owners))
            def _():
                remote(q_in.at[:, columns(peer, head)], q.at[own_rows], *sems)

            if rest:

                @pl.when((peer >= half) & (me == full))
                def _():
                    remote(
                        q_in.at[pl.ds(rest, rows - rest), columns(peer, head)],
                        q.at[pl.ds(PATCH, rows - rest)],
                        *sems,
                    )

            return carry

        lax.fori_loop(1, n, send_query, 0)

    def send_first(head, count):
        for kind, source in enumerate((q_in, k_in, v_in)):
            target = bufs[head][4 + kind]

            def send(peer, carry, kind=kind, source=source, target=target):
                part = source.at[pl.ds(0, count), columns(peer + half, head)]
                place = target.at[0, pl.ds(pl.multiple_of(me * rows, rows), count)]

                @pl.when(peer == me)
                def _():
                    local(part, place, x_recv.at[head, kind])

                @pl.when(peer != me)
                def _():
                    remote(part, place, x_send.at[head, kind], x_recv.at[head, kind], peer)

                return carry

            lax.fori_loop(0, half, send, 0)

    for head in range(heads):
        send_head(head)
        pl.when(me < full)(functools.partial(send_first, head, rows))
        if rest:
            pl.when(me == full)(functools.partial(send_first, head, rest))

    pltpu.make_async_copy(rank_in, rank, small_sem.at[0]).wait()
    pltpu.make_async_copy(ends_in, ends, small_sem.at[1]).wait()

    def first_of_partner(head):
        xq, xk, xv, xo = bufs[head][4:]
        for kind, ref in enumerate((xq, xk, xv)):
            wait_for(ref, x_recv.at[head, kind])
        attend(0, lambda block: 0, 1, rank, ends, xq.at[0], xk, xv, xo)
        for owner in range(owners):
            count = rows if owner < full else rest
            part = xo.at[pl.ds(owner * rows, count)]
            place = out.at[pl.ds(0, count), columns(me + half, head)]

            @pl.when(me == owner)
            def _():
                local(part, place, out_recv)

            @pl.when(me != owner)
            def _():
                remote(part, place, xo_send.at[head], out_recv, owner)

    for head in range(heads):
        q, k, v, o = bufs[head][:4]
        later = pl.ds(PATCH, q.shape[0] - PATCH)
        wait_for(k, recv_sem.at[head, 0])
        wait_for(v, recv_sem.at[head, 1])

        @pl.when(lower)
        def _():
            wait_for(q, recv_sem.at[head, 2])

        @pl.when(jnp.logical_not(lower))
        def _():
            wait_for(q.at[later], recv_sem.at[head, 2])

        def send_out(block, carry, head=head, o=o):
            source = o.at[pl.ds(pl.multiple_of(block * rows, rows), rows)]
            target = out.at[:, columns(me, head)]

            @pl.when(block == me)
            def _():
                local(source, target, out_recv)

            @pl.when((block != me) & (lower | (block >= owners)))
            def _():
                remote(source, target, out_send.at[head], out_recv, block)

            if rest:

                @pl.when(jnp.logical_not(lower) & (block == full))
                def _():
                    remote(
                        o.at[pl.ds(PATCH, rows - rest)],
                        out.at[pl.ds(rest, rows - rest), columns(me, head)],
                        out_send.at[head],
                        out_recv,
                        full,
                    )

            return carry

        @pl.when(lower)
        def _():
            attend(0, lambda block: 0, 1, rank, ends, q, k, v, o)
            lax.fori_loop(0, full, send_out, 0)

        def one_patch(patch, carry, q=q, k=k, v=v, o=o, send_out=send_out):
            mine = rank[patch]
            attend(
                patch,
                lambda block: (rank[block] > mine).astype(jnp.int32),
                patches,
                rank,
                ends,
                q,
                k,
                v,
                o,
            )
            lax.fori_loop(patch * PATCH // rows, (patch + 1) * PATCH // rows, send_out, 0)
            return carry

        lax.fori_loop(1, patches, one_patch, 0)
        if head == 0:

            @pl.when(lower)
            def _():
                for each in range(heads):
                    first_of_partner(each)

    def settle(ref, count, sem):
        part = ref.at[pl.ds(0, count)]
        wait_for(part, sem)

    for head in range(heads):
        q, k, v, o = bufs[head][:4]
        settle(q, (n - 1) * rows, send_sem.at[head, 0])
        settle(q, (n - 1) * rows, send_sem.at[head, 1])

        @pl.when(me < full)
        def _():
            settle(q, (half - 1) * rows, send_sem.at[head, 2])
            for kind in range(3):
                settle(q, (half - 1) * rows, x_send.at[head, kind])
            settle(q, PATCH - rows, xo_send.at[head])

        if rest:

            @pl.when(me == full)
            def _():
                settle(q, (n - 1) * rows - half * rest, send_sem.at[head, 2])
                for kind in range(3):
                    settle(q, (half - 1) * rest, x_send.at[head, kind])
                settle(q, PATCH - rest, xo_send.at[head])

        @pl.when(me >= owners)
        def _():
            settle(q, (n - 1) * rows, send_sem.at[head, 2])

        @pl.when(lower & (me >= owners))
        def _():
            settle(q, PATCH, xo_send.at[head])

        @pl.when(lower)
        def _():
            settle(o, (n - 1) * rows, out_send.at[head])

        @pl.when(jnp.logical_not(lower))
        def _():
            settle(o, (n - 1) * rows - PATCH, out_send.at[head])

    wait_for(out, out_recv)


def shards(n, q_fresh, k_fresh, v_fresh, k_stale, v_stale, rank, ends):
    rows, whole_width = q_fresh.shape
    heads = whole_width // n // HEAD_DIM
    span = n * rows
    hbm = pl.BlockSpec(memory_space=pltpu.HBM)
    scratch = []
    for _ in range(heads):
        scratch += [
            pltpu.VMEM((span, HEAD_DIM), jnp.bfloat16),
            pltpu.VMEM((2, span, HEAD_DIM), jnp.bfloat16),
            pltpu.VMEM((2, span, HEAD_DIM), jnp.bfloat16),
            pltpu.VMEM((span, HEAD_DIM), jnp.bfloat16),
            pltpu.VMEM((1, PATCH, HEAD_DIM), jnp.bfloat16),
            pltpu.VMEM((1, PATCH, HEAD_DIM), jnp.bfloat16),
            pltpu.VMEM((1, PATCH, HEAD_DIM), jnp.bfloat16),
            pltpu.VMEM((PATCH, HEAD_DIM), jnp.bfloat16),
        ]
    scratch += [
        pltpu.SMEM(rank.shape, jnp.int32),
        pltpu.SMEM(ends.shape, jnp.int32),
        pltpu.SemaphoreType.DMA((2,)),
        pltpu.SemaphoreType.DMA((heads, 3)),
        pltpu.SemaphoreType.DMA((heads, 3)),
        pltpu.SemaphoreType.DMA((heads, 3)),
        pltpu.SemaphoreType.DMA((heads, 3)),
        pltpu.SemaphoreType.DMA((heads,)),
        pltpu.SemaphoreType.DMA((heads,)),
        pltpu.SemaphoreType.DMA,
    ]
    return pl.pallas_call(
        functools.partial(kernel, n, heads),
        out_shape=jax.ShapeDtypeStruct(q_fresh.shape, q_fresh.dtype),
        in_specs=[hbm] * 7,
        out_specs=hbm,
        scratch_shapes=scratch,
        compiler_params=pltpu.CompilerParams(
            collective_id=0, has_side_effects=True, vmem_limit_bytes=62 * 1024 * 1024
        ),
        cost_estimate=pl.CostEstimate(
            flops=4 * heads * span * span * HEAD_DIM,
            bytes_accessed=12 * rows * whole_width,
            transcendentals=heads * span * span,
        ),
    )(q_fresh, k_fresh, v_fresh, k_stale, v_stale, rank, ends)


def solution(mesh):
    return jax.shard_map(
        functools.partial(shards, mesh.shape["seq"]),
        mesh=mesh,
        in_specs=(
            P(("groups", "seq"), None),
            P(("groups", "seq"), None),
            P(("groups", "seq"), None),
            P("groups", "seq"),
            P("groups", "seq"),
            P("groups"),
            P("groups"),
        ),
        out_specs=P(("groups", "seq"), None),
        check_vma=False,
    )
```

time: 125 us -> 117 us (0.936)
  Pallas kernels: 118 us -> 114 us
  local copies, waits for them, and re-layouts: 6.32 us -> 2.49 us
    pallas_call x1, Pallas kernels: 118 us -> 114 us  [shards(): pl.pallas_call(functools.partial(kernel, n, heads), out_shape=jax.ShapeDt...]
    unnamed x11 -> x1, local copies, waits for them, and re-layouts: 6.32 us -> 2.49 us
where the time goes in v2:
time: 117 us; the launch traced here: 116 us
  Pallas kernels  114 us (97%)
  local copies, waits for them, and re-layouts  2.49 us (2%)
    pallas_call x1, Pallas kernels, shards(): pl.pallas_call(functools.partial(kernel, n, heads), out_shape=jax.ShapeDt...  114 us
    unnamed x1, local copies, waits for them, and re-layouts  2.49 us

profile of v2, /device:TPU:13, one launch (start us, length us, event | category | flops | bytes accessed | tf_op | source)
XLA Modules:
  0.0 116.1 jit_solution(11286598544999518621)
XLA Ops:
  0.0 113.6 %shard_map.73 = bf16[160,4096]{1,0:T(8,128)(2,1)} custom-call(bf16[160,4096]{1,0:T(8,128)(2,1)} %q_in.1, bf16[160,4096]{1,0:T(8,128)(2,1)} %k_in.1, bf16[160,4096]{1,0:T(8,128)(2,1)} %v_in.1, bf16[2560,256]{1,0:T(8,128)(2,1)} %ks_in.1, bf16[2560,256]{1,0:T(8,128)(2,1)} %vs_in.1, s32[5]{0:T(128)} %rank_in.1, s32[5]{0:T(128)} %ends_in.1), custom_call_target="tpu_custom_call" | custom-call | flops 6710886400 | bytes 7864320 | tf_op jit(solution)/shard_map/pallas_call | solution.py:326
  113.6 2.5 %copy.9 = bf16[160,4096]{1,0:T(8,128)(2,1)} copy(bf16[160,4096]{1,0:T(8,128)(2,1)} %shard_map.73) | data formatting | bytes 2621440

commit v3 on v2

--- a/solution.py
+++ b/solution.py
@@ -154,11 +154,13 @@
 
             lax.fori_loop(0, half, send, 0)
 
-    for head in range(heads):
-        send_head(head)
+    send_head(0)
+    for head in range(heads):
         pl.when(me < full)(functools.partial(send_first, head, rows))
         if rest:
             pl.when(me == full)(functools.partial(send_first, head, rest))
+    for head in range(1, heads):
+        send_head(head)
 
     pltpu.make_async_copy(rank_in, rank, small_sem.at[0]).wait()
     pltpu.make_async_copy(ends_in, ends, small_sem.at[1]).wait()
@@ -181,6 +183,33 @@
             def _():
                 remote(part, place, xo_send.at[head], out_recv, owner)
 
+    def send_out(head, block, carry):
+        o = bufs[head][3]
+        source = o.at[pl.ds(pl.multiple_of(block * rows, rows), rows)]
+        target = out.at[:, columns(me, head)]
+
+        @pl.when(block == me)
+        def _():
+            local(source, target, out_recv)
+
+        @pl.when((block != me) & (lower | (block >= owners)))
+        def _():
+            remote(source, target, out_send.at[head], out_recv, block)
+
+        if rest:
+
+            @pl.when(jnp.logical_not(lower) & (block == full))
+            def _():
+                remote(
+                    o.at[pl.ds(PATCH, rows - rest)],
+                    out.at[pl.ds(rest, rows - rest), columns(me, head)],
+                    out_send.at[head],
+                    out_recv,
+                    full,
+                )
+
+        return carry
+
     for head in range(heads):
         q, k, v, o = bufs[head][:4]
         later = pl.ds(PATCH, q.shape[0] - PATCH)
@@ -195,38 +224,10 @@
         def _():
             wait_for(q.at[later], recv_sem.at[head, 2])
 
-        def send_out(block, carry, head=head, o=o):
-            source = o.at[pl.ds(pl.multiple_of(block * rows, rows), rows)]
-            target = out.at[:, columns(me, head)]
-
-            @pl.when(block == me)
-            def _():
-                local(source, target, out_recv)
-
-            @pl.when((block != me) & (lower | (block >= owners)))
-            def _():
-                remote(source, target, out_send.at[head], out_recv, block)
-
-            if rest:
-
-                @pl.when(jnp.logical_not(lower) & (block == full))
-                def _():
-                    remote(
-                        o.at[pl.ds(PATCH, rows - rest)],
-                        out.at[pl.ds(rest, rows - rest), columns(me, head)],
-                        out_send.at[head],
-                        out_recv,
-                        full,
-                    )
-
-            return carry
-
-        @pl.when(lower)
-        def _():
-            attend(0, lambda block: 0, 1, rank, ends, q, k, v, o)
-            lax.fori_loop(0, full, send_out, 0)
-
-        def one_patch(patch, carry, q=q, k=k, v=v, o=o, send_out=send_out):
+        send = functools.partial(send_out, head)
+
+        def one_patch(step, carry, q=q, k=k, v=v, o=o, send=send):
+            patch = jnp.where(lower, patches - step, step)
             mine = rank[patch]
             attend(
                 patch,
@@ -239,10 +240,25 @@
                 v,
                 o,
             )
-            lax.fori_loop(patch * PATCH // rows, (patch + 1) * PATCH // rows, send_out, 0)
+            start, stop = patch * PATCH, (patch + 1) * PATCH
+
+            @pl.when(lower)
+            def _():
+                lax.fori_loop((start + rows - 1) // rows, (stop + rows - 1) // rows, send, 0)
+
+            @pl.when(jnp.logical_not(lower))
+            def _():
+                lax.fori_loop(jnp.maximum(start // rows, half), stop // rows, send, 0)
+
             return carry
 
         lax.fori_loop(1, patches, one_patch, 0)
+
+        @pl.when(lower)
+        def _():
+            attend(0, lambda block: 0, 1, rank, ends, q, k, v, o)
+            lax.fori_loop(0, owners, send, 0)
+
         if head == 0:
 
             @pl.when(lower)
@@ -255,13 +271,34 @@
         wait_for(part, sem)
 
     for head in range(heads):
-        q, k, v, o = bufs[head][:4]
+        q = bufs[head][0]
         settle(q, (n - 1) * rows, send_sem.at[head, 0])
         settle(q, (n - 1) * rows, send_sem.at[head, 1])
 
         @pl.when(me < full)
         def _():
             settle(q, (half - 1) * rows, send_sem.at[head, 2])
+
+        if rest:
+
+            @pl.when(me == full)
+            def _():
+                settle(q, (n - 1) * rows - half * rest, send_sem.at[head, 2])
+
+        @pl.when(me >= owners)
+        def _():
+            settle(q, (n - 1) * rows, send_sem.at[head, 2])
+
+    @pl.when(jnp.logical_not(lower))
+    def _():
+        for head in range(heads):
+            lax.fori_loop(full, half, functools.partial(send_out, head), 0)
+
+    for head in range(heads):
+        q, k, v, o = bufs[head][:4]
+
+        @pl.when(me < full)
+        def _():
             for kind in range(3):
                 settle(q, (half - 1) * rows, x_send.at[head, kind])
             settle(q, PATCH - rows, xo_send.at[head])
@@ -270,14 +307,9 @@
 
             @pl.when(me == full)
             def _():
-                settle(q, (n - 1) * rows - half * rest, send_sem.at[head, 2])
                 for kind in range(3):
                     settle(q, (half - 1) * rest, x_send.at[head, kind])
                 settle(q, PATCH - rest, xo_send.at[head])
-
-        @pl.when(me >= owners)
-        def _():
-            settle(q, (n - 1) * rows, send_sem.at[head, 2])
 
         @pl.when(lower & (me >= owners))
         def _():

time: 117 us -> 115 us (0.983)
  no operation moved by 1% of the time
where the time goes in v3:
time: 115 us
  Pallas kernels  113 us (98%)
  local copies, waits for them, and re-layouts  2.49 us (2%)
    pallas_call x1, Pallas kernels, shards(): pl.pallas_call(functools.partial(kernel, n, heads), out_shape=jax.ShapeDt...  113 us
    unnamed x1, local copies, waits for them, and re-layouts  2.49 us

profile of v3, /device:TPU:13, one launch (start us, length us, event | category | flops | bytes accessed | tf_op | source)
XLA Modules:
  0.0 115.3 jit_solution(6845757863486073270)
XLA Ops:
  0.0 112.8 %shard_map.73 = bf16[160,4096]{1,0:T(8,128)(2,1)} custom-call(bf16[160,4096]{1,0:T(8,128)(2,1)} %q_in.1, bf16[160,4096]{1,0:T(8,128)(2,1)} %k_in.1, bf16[160,4096]{1,0:T(8,128)(2,1)} %v_in.1, bf16[2560,256]{1,0:T(8,128)(2,1)} %ks_in.1, bf16[2560,256]{1,0:T(8,128)(2,1)} %vs_in.1, s32[5]{0:T(128)} %rank_in.1, s32[5]{0:T(128)} %ends_in.1), custom_call_target="tpu_custom_call" | custom-call | flops 6710886400 | bytes 7864320 | tf_op jit(solution)/shard_map/pallas_call | solution.py:358
  112.8 2.5 %copy.9 = bf16[160,4096]{1,0:T(8,128)(2,1)} copy(bf16[160,4096]{1,0:T(8,128)(2,1)} %shard_map.73) | data formatting | bytes 2621440
